TPU v7x, 256 devices: a whole 4x4x8 slice. The times are simulated.
256 devices in a mesh: sub: 128 (over x, z_hi, y, core), rng: 2 (over z_lo).
Axes of the slice: x: 4, y: 4, z: 8 (z_hi: 4, z_lo: 2; z = z_hi * 2 + z_lo), core: 2. Of those that a mesh axis runs over, the one named last changes fastest.
Arguments:
- image: float32 [2, 16384, 2048], P(None, 'sub', 'rng'), may hold values from -6 to 6
- angle_offset: int32 [4, 2, 128], P(None, None, 'sub'), may hold values from -2 to 2
- angle_fraction: float32 [4, 2, 16384], P(None, None, 'sub'), may hold values from -0.5 to 0.5
- integer_distance_shifts: int32 [4, 2, 128], P(None, None, 'sub'), may hold values from -59 to 59
- subcell_distance_shares: float32 [4, 2, 16384], P(None, None, 'sub'), may hold values from -0.5 to 0.5
Outputs:
- merged: float32 [2, 16384, 2048], P(None, 'sub', 'rng')
All inputs are finite; a program needn't handle non-finite values.
Results may differ from a plain program's by a relative error of at most 0.0003.
Values sent between devices are 32-bit elements; how exact they have to be, the bound alone decides.
A program may use at most 64 MiB of HBM per device.

v0:
```python
import jax
import jax.numpy as jnp
from jax import lax
from jax.sharding import PartitionSpec as P

HALO = 64
LEVELS = 4


frequency_quotient = 3.7


def extended(cells, sides, width):
    for axis, dim in sides:
        count = lax.axis_size(axis)
        ends = count - 1
        head = lax.slice_in_dim(cells, 0, width, axis=dim)
        tail = lax.slice_in_dim(cells, cells.shape[dim] - width, cells.shape[dim], axis=dim)
        cells = jnp.concatenate(
            [
                lax.ppermute(tail, axis, [(i, (i + 1) % count) for i in range(ends)]),
                cells,
                lax.ppermute(head, axis, [((i + 1) % count, i) for i in range(ends)]),
            ],
            axis=dim,
        )
    return cells


def from_partner(x, axis, distance):
    return lax.ppermute(x, axis, [(i, i ^ 1 << distance) for i in range(lax.axis_size(axis))])


def keys_kernel(sample_displacement):
    magnitude = jnp.abs(sample_displacement)
    inner_part = (1.5 * magnitude - 2.5) * magnitude * magnitude + 1.0
    outer_part = ((-0.5 * magnitude + 2.5) * magnitude - 4.0) * magnitude + 2.0
    return jnp.where(magnitude < 1.0, inner_part, jnp.where(magnitude < 2.0, outer_part, 0.0))


def sinc_taper(sample_displacement):
    window = 0.54 + 0.46 * jnp.cos(jnp.pi * sample_displacement / 4.0)
    return jnp.where(
        jnp.abs(sample_displacement) < 4.0, jnp.sinc(sample_displacement) * window, 0.0
    )


def range_shift(tile_block, sample_displacement, fraction):
    output_breadth = tile_block.shape[-1] - 2 * HALO
    start = HALO - 4 + sample_displacement
    window = lax.dynamic_slice_in_dim(tile_block, start, output_breadth + 8, 2)
    summed = jnp.zeros(tile_block.shape[:2] + (output_breadth,), jnp.float32)
    for shift_tap in range(9):
        weight = sinc_taper(shift_tap - 4 - fraction)
        summed = (
            summed + weight[None, :, None] * window[:, :, shift_tap : shift_tap + output_breadth]
        )
    return summed


def child_term(
    child,
    upper_half,
    angle_offset,
    angle_fraction,
    integer_distance_shifts,
    subcell_distance_shares,
):
    beam_count = child.shape[1]
    tile_count = angle_offset.shape[0]
    parent_group_span = beam_count // tile_count
    parent = jnp.arange(beam_count).astype(jnp.float32)
    column = jnp.arange(beam_count).astype(jnp.float32)
    position = 0.5 * (upper_half.astype(jnp.float32) * beam_count + parent)
    position = (
        position + jnp.repeat(angle_offset, parent_group_span).astype(jnp.float32) + angle_fraction
    )
    weights = keys_kernel(column[None, :] - position[:, None])
    steered = jnp.einsum("ij,pjr->pir", weights, child, precision=lax.Precision.HIGHEST)
    image_groups = steered.reshape(2, tile_count, parent_group_span, steered.shape[-1])
    shifted = jax.vmap(range_shift, in_axes=(1, 0, 0), out_axes=1)(
        image_groups,
        integer_distance_shifts,
        subcell_distance_shares.reshape(tile_count, parent_group_span),
    )
    shifted = shifted.reshape(2, beam_count, shifted.shape[-1])
    viewing_bearing = (
        frequency_quotient
        * jnp.pi
        * (
            jnp.repeat(integer_distance_shifts, parent_group_span).astype(jnp.float32)
            + subcell_distance_shares
        )
    )
    cosine = jnp.cos(viewing_bearing)[:, None]
    sine_part = jnp.sin(viewing_bearing)[:, None]
    return jnp.stack(
        [cosine * shifted[0] - sine_part * shifted[1], sine_part * shifted[0] + cosine * shifted[1]]
    )


def merge_pair(
    children,
    upper_half,
    angle_offset,
    angle_fraction,
    integer_distance_shifts,
    subcell_distance_shares,
):
    summed = None
    for which in range(2):
        rotated = child_term(
            children[which],
            upper_half,
            angle_offset[which],
            angle_fraction[which],
            integer_distance_shifts[which],
            subcell_distance_shares[which],
        )
        summed = rotated if summed is None else summed + rotated
    return summed * 0.70710678


def per_device(
    image, angle_offset, angle_fraction, integer_distance_shifts, subcell_distance_shares
):
    current = image
    for level in range(LEVELS):
        upper_half = jnp.bitwise_and(jnp.right_shift(lax.axis_index("sub"), level), 1)
        own_image = extended(current, (("rng", 2),), HALO)
        partner_image = from_partner(own_image, "sub", level)
        child_low = jnp.where(upper_half == 0, own_image, partner_image)
        child_high = jnp.where(upper_half == 0, partner_image, own_image)
        current = merge_pair(
            (child_low, child_high),
            upper_half,
            angle_offset[level],
            angle_fraction[level],
            integer_distance_shifts[level],
            subcell_distance_shares[level],
        )
    return current


def solution(mesh):
    placed = (
        P(None, "sub", "rng"),
        P(None, None, "sub"),
        P(None, None, "sub"),
        P(None, None, "sub"),
        P(None, None, "sub"),
    )
    return jax.shard_map(
        per_device, mesh=mesh, in_specs=placed, out_specs=P(None, "sub", "rng"), check_vma=False
    )
```

profile of v0, /device:TPU:6, one launch (start us, length us, event | category | flops | bytes accessed | tf_op | source)
XLA Modules:
  0.0 186.5 jit_solution(2513243593645687845)
XLA Ops:
  1.1 3.8 %collective-permute-start = (f32[2,128,64]{2,1,0:T(8,128)S(1)}, f32[2,128,64]{2,1,0:T(8,128)S(1)}, u32[]{:S(2)}, u32[]{:S(2)}) collective-permute-start(f32[2,128,64]{2,1,0:T(8,128)S(1)} %get-tuple-element.117), channel_id=1, source_target_pairs={{0,1},{2,3},{4,5},{6,7},{8,9},{10,11},{12,13},{14,15},{16,17},{18,... | collective-permute-start | bytes 196616 | tf_op jit(solution)/shard_map/ppermute | solution.py:21
  5.0 1.4 collective-permute-start.1
  7.6 4.3 %collective-permute-done.1 = f32[2,128,64]{2,1,0:T(8,128)S(1)} collective-permute-done((f32[2,128,64]{2,1,0:T(8,128)S(1)}, f32[2,128,64]{2,1,0:T(8,128)S(1)}, u32[]{:S(2)}, u32[]{:S(2)}) %collective-permute-start.1) | collective-permute-done | bytes 65568 | tf_op jit(solution)/shard_map/ppermute | solution.py:23
  11.9 1.7 concatenate.36
  30.3 2.0 %fusion.12 = f32[2,1152,128]{2,1,0:T(8,128)S(1)} fusion(f32[2,128,1152]{2,1,0:T(8,128)S(1)} %collective-permute-done.2, f32[2,128,1152]{2,1,0:T(8,128)S(1)} %concatenate.36, pred[]{:T(512)S(6)} %eq.31, f32[128]{0:T(128)S(1)} %get-tuple-element.211, f32[128]{0:T(128)S(1)} %iota_convert_fusion), kind=kOutput, calls=%fused_computation.15 | convolution fusion | flops 453558272 | bytes 3539969 | tf_op jit(solution)/shard_map/ij,pjr->pir/dot_general | solution.py:79
  32.4 2.0 %fusion.14 = f32[2,1152,128]{2,1,0:T(8,128)S(1)} fusion(f32[2,128,1152]{2,1,0:T(8,128)S(1)} %concatenate.36, f32[2,128,1152]{2,1,0:T(8,128)S(1)} %collective-permute-done.2, pred[]{:T(512)S(6)} %eq.31, f32[128]{0:T(128)S(1)} %get-tuple-element.212, f32[128]{0:T(128)S(1)} %iota_convert_fusion), kind=kOutput, calls=%fused_computation.17 | convolution fusion | flops 453558272 | bytes 3539969 | tf_op jit(solution)/shard_map/ij,pjr->pir/dot_general | solution.py:79
  37.1 1.5 collective-permute-start.3
  38.6 1.3 collective-permute-start.4
  40.7 4.1 %collective-permute-done.4 = f32[2,128,64]{1,2,0:T(8,128)S(1)} collective-permute-done((f32[2,128,64]{1,2,0:T(8,128)S(1)}, f32[2,128,64]{1,2,0:T(8,128)S(1)}, u32[]{:S(2)}, u32[]{:S(2)}) %collective-permute-start.4) | collective-permute-done | bytes 65568 | tf_op jit(solution)/shard_map/ppermute | solution.py:23
  44.9 1.8 collective-permute-start.5
  50.0 22.5 %collective-permute-done.5 = f32[2,128,1152]{1,2,0:T(8,128)S(1)} collective-permute-done((f32[2,128,1152]{1,2,0:T(8,128)S(1)}, f32[2,128,1152]{1,2,0:T(8,128)S(1)}, u32[]{:S(2)}, u32[]{:S(2)}) %collective-permute-start.5) | collective-permute-done | bytes 1179680 | tf_op jit(solution)/shard_map/ppermute | solution.py:31
  72.5 1.9 %fusion.8 = f32[2,1152,128]{2,1,0:T(8,128)S(1)} fusion(f32[2,128,1152]{1,2,0:T(8,128)S(1)} %collective-permute-done.5, pred[]{:T(512)S(6)} %eq.30, f32[128]{0:T(128)} %get-tuple-element.209, f32[128]{0:T(128)S(1)} %iota_convert_fusion, f32[2,128,64]{1,2,0:T(8,128)S(1)} %collective-permute-done.4, f32[2,128,1024]{1,2,0:T(8,128)S(1)} %fusion.80, ...), kind=kOutput, calls=%fused_computation.11 | convolution fusion | flops 454148096 | bytes 3539969 | tf_op jit(solution)/shard_map/ij,pjr->pir/dot_general | solution.py:79
  80.2 1.5 collective-permute-start.6
  81.7 1.3 collective-permute-start.7
  83.6 4.3 %collective-permute-done.7 = f32[2,128,64]{1,2,0:T(8,128)S(1)} collective-permute-done((f32[2,128,64]{1,2,0:T(8,128)S(1)}, f32[2,128,64]{1,2,0:T(8,128)S(1)}, u32[]{:S(2)}, u32[]{:S(2)}) %collective-permute-start.7) | collective-permute-done | bytes 65568 | tf_op jit(solution)/shard_map/ppermute | solution.py:23
  88.0 3.5 %collective-permute-start.8 = (f32[2,128,1152]{1,2,0:T(8,128)S(1)}, f32[2,128,1152]{1,2,0:T(8,128)S(1)}, u32[]{:S(2)}, u32[]{:S(2)}) collective-permute-start(f32[2,128,1152]{1,2,0:T(8,128)S(1)} %pad_maximum_fusion.1), channel_id=1, source_target_pairs={{0,8},{2,10},{4,12},{6,14},{8,0},{10,2},{12,4},{14,6},{16,24},{18,... | collective-permute-start | bytes 3538952 | tf_op jit(solution)/shard_map/ppermute | solution.py:31
  95.7 19.1 %collective-permute-done.8 = f32[2,128,1152]{1,2,0:T(8,128)S(1)} collective-permute-done((f32[2,128,1152]{1,2,0:T(8,128)S(1)}, f32[2,128,1152]{1,2,0:T(8,128)S(1)}, u32[]{:S(2)}, u32[]{:S(2)}) %collective-permute-start.8) | collective-permute-done | bytes 1179680 | tf_op jit(solution)/shard_map/ppermute | solution.py:31
  114.9 1.8 fusion.4
  121.2 1.3 collective-permute-start.10
  122.5 4.5 %collective-permute-start.9 = (f32[2,128,64]{1,2,0:T(8,128)S(1)}, f32[2,128,64]{1,2,0:T(8,128)S(1)}, u32[]{:S(2)}, u32[]{:S(2)}) collective-permute-start(f32[2,128,64]{1,2,0:T(8,128)S(1)} %get-tuple-element.110), channel_id=1, source_target_pairs={{0,1},{2,3},{4,5},{6,7},{8,9},{10,11},{12,13},{14,15},{16,17},{18,... | collective-permute-start | bytes 196616 | tf_op jit(solution)/shard_map/ppermute | solution.py:21
  127.4 2.2 %collective-permute-done.9 = f32[2,128,64]{1,2,0:T(8,128)S(1)} collective-permute-done((f32[2,128,64]{1,2,0:T(8,128)S(1)}, f32[2,128,64]{1,2,0:T(8,128)S(1)}, u32[]{:S(2)}, u32[]{:S(2)}) %collective-permute-start.9) | collective-permute-done | bytes 65568 | tf_op jit(solution)/shard_map/ppermute | solution.py:21
  129.6 3.3 %collective-permute-start.11 = (f32[2,128,1152]{1,2,0:T(8,128)S(1)}, f32[2,128,1152]{1,2,0:T(8,128)S(1)}, u32[]{:S(2)}, u32[]{:S(2)}) collective-permute-start(f32[2,128,1152]{1,2,0:T(8,128)S(1)} %pad_maximum_fusion.2), channel_id=1, source_target_pairs={{0,16},{2,18},{4,20},{6,22},{8,24},{10,26},{12,28},{14,30},{16,0},... | collective-permute-start | bytes 3538952 | tf_op jit(solution)/shard_map/ppermute | solution.py:31
  136.0 43.3 %collective-permute-done.11 = f32[2,128,1152]{1,2,0:T(8,128)S(1)} collective-permute-done((f32[2,128,1152]{1,2,0:T(8,128)S(1)}, f32[2,128,1152]{1,2,0:T(8,128)S(1)}, u32[]{:S(2)}, u32[]{:S(2)}) %collective-permute-start.11) | collective-permute-done | bytes 1179680 | tf_op jit(solution)/shard_map/ppermute | solution.py:31
  185.2 1.3 copy.8
  (161 shorter events, 29.5 us)
Async XLA Ops:
  1.1 6.6 %collective-permute-start = (f32[2,128,64]{2,1,0:T(8,128)S(1)}, f32[2,128,64]{2,1,0:T(8,128)S(1)}, u32[]{:S(2)}, u32[]{:S(2)}) collective-permute-start(f32[2,128,64]{2,1,0:T(8,128)S(1)} %get-tuple-element.117), channel_id=1, source_target_pairs={{0,1},{2,3},{4,5},{6,7},{8,9},{10,11},{12,13},{14,15},{16,17},{18,... | collective-permute-start | bytes 196616 | tf_op jit(solution)/shard_map/ppermute | solution.py:21
  4.9 8.9 %copy-start.1 = (s32[4,2,1]{0,2,1:T(1,128)S(1)}, s32[4,2,1]{0,2,1:T(1,128)}, u32[]{:S(2)}) copy-start(s32[4,2,1]{0,2,1:T(1,128)} %param.9) | copy-start | bytes 100
  4.9 13.5 %copy-start.2 = (s32[4,2,1]{0,2,1:T(1,128)S(1)}, s32[4,2,1]{0,2,1:T(1,128)}, u32[]{:S(2)}) copy-start(s32[4,2,1]{0,2,1:T(1,128)} %param.7) | copy-start | bytes 100
  4.9 22.3 %copy-start.3 = (f32[4,2,128]{2,1,0:T(2,128)S(1)}, f32[4,2,128]{2,1,0:T(2,128)}, u32[]{:S(2)}) copy-start(f32[4,2,128]{2,1,0:T(2,128)} %param.8) | copy-start | bytes 12292
  4.9 22.9 %copy-start = (f32[4,2,128]{2,1,0:T(2,128)S(1)}, f32[4,2,128]{2,1,0:T(2,128)}, u32[]{:S(2)}) copy-start(f32[4,2,128]{2,1,0:T(2,128)} %param.10) | copy-start | bytes 12292
  5.0 7.0 %collective-permute-start.1 = (f32[2,128,64]{2,1,0:T(8,128)S(1)}, f32[2,128,64]{2,1,0:T(8,128)S(1)}, u32[]{:S(2)}, u32[]{:S(2)}) collective-permute-start(f32[2,128,64]{2,1,0:T(8,128)S(1)} %get-tuple-element.116), channel_id=1, source_target_pairs={{1,0},{3,2},{5,4},{7,6},{9,8},{11,10},{13,12},{15,14},{17,16},{19,... | collective-permute-start | bytes 196616 | tf_op jit(solution)/shard_map/ppermute | solution.py:23
  13.7 16.6 %collective-permute-start.2 = (f32[2,128,1152]{2,1,0:T(8,128)S(1)}, f32[2,128,1152]{2,1,0:T(8,128)S(1)}, u32[]{:S(2)}, u32[]{:S(2)}) collective-permute-start(f32[2,128,1152]{2,1,0:T(8,128)S(1)} %concatenate.36), channel_id=1, source_target_pairs={{0,2},{2,0},{4,6},{6,4},{8,10},{10,8},{12,14},{14,12},{16,18},{18,... | collective-permute-start | bytes 3538952 | tf_op jit(solution)/shard_map/ppermute | solution.py:31
  37.1 3.6 %collective-permute-start.3 = (f32[2,128,64]{1,2,0:T(8,128)S(1)}, f32[2,128,64]{1,2,0:T(8,128)S(1)}, u32[]{:S(2)}, u32[]{:S(2)}) collective-permute-start(f32[2,128,64]{1,2,0:T(8,128)S(1)} %get-tuple-element.114), channel_id=1, source_target_pairs={{0,1},{2,3},{4,5},{6,7},{8,9},{10,11},{12,13},{14,15},{16,17},{18,... | collective-permute-start | bytes 196616 | tf_op jit(solution)/shard_map/ppermute | solution.py:21
  38.6 6.2 %collective-permute-start.4 = (f32[2,128,64]{1,2,0:T(8,128)S(1)}, f32[2,128,64]{1,2,0:T(8,128)S(1)}, u32[]{:S(2)}, u32[]{:S(2)}) collective-permute-start(f32[2,128,64]{1,2,0:T(8,128)S(1)} %get-tuple-element.115), channel_id=1, source_target_pairs={{1,0},{3,2},{5,4},{7,6},{9,8},{11,10},{13,12},{15,14},{17,16},{19,... | collective-permute-start | bytes 196616 | tf_op jit(solution)/shard_map/ppermute | solution.py:23
  44.9 27.6 %collective-permute-start.5 = (f32[2,128,1152]{1,2,0:T(8,128)S(1)}, f32[2,128,1152]{1,2,0:T(8,128)S(1)}, u32[]{:S(2)}, u32[]{:S(2)}) collective-permute-start(f32[2,128,1152]{1,2,0:T(8,128)S(1)} %pad_maximum_fusion), channel_id=1, source_target_pairs={{0,4},{2,6},{4,0},{6,2},{8,12},{10,14},{12,8},{14,10},{16,20},{18,... | collective-permute-start | bytes 3538952 | tf_op jit(solution)/shard_map/ppermute | solution.py:31
  77.0 1.2 copy-start.45
  77.0 1.2 copy-start.46
  80.2 3.4 %collective-permute-start.6 = (f32[2,128,64]{1,2,0:T(8,128)S(1)}, f32[2,128,64]{1,2,0:T(8,128)S(1)}, u32[]{:S(2)}, u32[]{:S(2)}) collective-permute-start(f32[2,128,64]{1,2,0:T(8,128)S(1)} %get-tuple-element.112), channel_id=1, source_target_pairs={{0,1},{2,3},{4,5},{6,7},{8,9},{10,11},{12,13},{14,15},{16,17},{18,... | collective-permute-start | bytes 196616 | tf_op jit(solution)/shard_map/ppermute | solution.py:21
  81.7 6.2 %collective-permute-start.7 = (f32[2,128,64]{1,2,0:T(8,128)S(1)}, f32[2,128,64]{1,2,0:T(8,128)S(1)}, u32[]{:S(2)}, u32[]{:S(2)}) collective-permute-start(f32[2,128,64]{1,2,0:T(8,128)S(1)} %get-tuple-element.113), channel_id=1, source_target_pairs={{1,0},{3,2},{5,4},{7,6},{9,8},{11,10},{13,12},{15,14},{17,16},{19,... | collective-permute-start | bytes 196616 | tf_op jit(solution)/shard_map/ppermute | solution.py:23
  88.0 26.9 %collective-permute-start.8 = (f32[2,128,1152]{1,2,0:T(8,128)S(1)}, f32[2,128,1152]{1,2,0:T(8,128)S(1)}, u32[]{:S(2)}, u32[]{:S(2)}) collective-permute-start(f32[2,128,1152]{1,2,0:T(8,128)S(1)} %pad_maximum_fusion.1), channel_id=1, source_target_pairs={{0,8},{2,10},{4,12},{6,14},{8,0},{10,2},{12,4},{14,6},{16,24},{18,... | collective-permute-start | bytes 3538952 | tf_op jit(solution)/shard_map/ppermute | solution.py:31
  121.2 6.2 %collective-permute-start.10 = (f32[2,128,64]{1,2,0:T(8,128)S(1)}, f32[2,128,64]{1,2,0:T(8,128)S(1)}, u32[]{:S(2)}, u32[]{:S(2)}) collective-permute-start(f32[2,128,64]{1,2,0:T(8,128)S(1)} %get-tuple-element.111), channel_id=1, source_target_pairs={{1,0},{3,2},{5,4},{7,6},{9,8},{11,10},{13,12},{15,14},{17,16},{19,... | collective-permute-start | bytes 196616 | tf_op jit(solution)/shard_map/ppermute | solution.py:23
  122.5 7.0 %collective-permute-start.9 = (f32[2,128,64]{1,2,0:T(8,128)S(1)}, f32[2,128,64]{1,2,0:T(8,128)S(1)}, u32[]{:S(2)}, u32[]{:S(2)}) collective-permute-start(f32[2,128,64]{1,2,0:T(8,128)S(1)} %get-tuple-element.110), channel_id=1, source_target_pairs={{0,1},{2,3},{4,5},{6,7},{8,9},{10,11},{12,13},{14,15},{16,17},{18,... | collective-permute-start | bytes 196616 | tf_op jit(solution)/shard_map/ppermute | solution.py:21
  129.6 49.6 %collective-permute-start.11 = (f32[2,128,1152]{1,2,0:T(8,128)S(1)}, f32[2,128,1152]{1,2,0:T(8,128)S(1)}, u32[]{:S(2)}, u32[]{:S(2)}) collective-permute-start(f32[2,128,1152]{1,2,0:T(8,128)S(1)} %pad_maximum_fusion.2), channel_id=1, source_target_pairs={{0,16},{2,18},{4,20},{6,22},{8,24},{10,26},{12,28},{14,30},{16,0},... | collective-permute-start | bytes 3538952 | tf_op jit(solution)/shard_map/ppermute | solution.py:31
  182.5 1.2 copy-start.9
  182.5 1.2 copy-start.10
  182.5 1.2 copy-start.11
  182.5 1.2 copy-start.12
  182.5 1.2 copy-start.13
  182.5 1.2 copy-start.32
  (41 other events, 32.3 us)
where the time goes:
time: 187 us; the launch traced here: 186 us
  waiting for transfers between devices  103 us (55%)
  starting transfers between devices  25.4 us (14%)
  between operations  21.1 us (11%)
  other arithmetic  15.8 us (8%)
  matrix products  12.5 us (7%)
  local copies, waits for them, and re-layouts  9.06 us (5%)
    ppermute x4, waiting for transfers between devices, from_partner(): lax.ppermute(x, axis, [(i, i ^ 1 << distance) for i in range(lax.axis_siz...  84.9 us
    ppermute x4, waiting for transfers between devices, extended(): lax.ppermute(head, axis, [((i + 1) % count, i) for i in range(ends)])  13 us
    dot_general x8, matrix products, child_term(): jnp.einsum('ij,pjr->pir', weights, child, precision=lax.Precision.HIGHEST)  12.5 us
    ppermute x4, starting transfers between devices, extended(): lax.ppermute(tail, axis, [(i, (i + 1) % count) for i in range(ends)])  11.4 us
    ppermute x4, starting transfers between devices, from_partner(): lax.ppermute(x, axis, [(i, i ^ 1 << distance) for i in range(lax.axis_siz...  8.74 us
    add x8, other arithmetic, range_shift(): summed + weight[None, :, None] * window[:, :, shift_tap:shift_tap + outpu...  8.44 us
    ppermute x4, starting transfers between devices, extended(): lax.ppermute(head, axis, [((i + 1) % count, i) for i in range(ends)])  5.3 us
    ppermute x4, waiting for transfers between devices, extended(): lax.ppermute(tail, axis, [(i, (i + 1) % count) for i in range(ends)])  4.76 us
  transfers between devices with their start and end apart: 12, of which 11 were waited for; matrix products, arithmetic and copies ran while one was open for 4% of the time, Pallas kernels for 0%

commit v1 on v0

v1 whole, which is shorter than its diff:
```python
import math

import jax
import jax.numpy as jnp
from jax import lax
from jax.experimental import pallas as pl
from jax.experimental.pallas import tpu as pltpu
from jax.sharding import PartitionSpec as P

LEVELS = 4
BEAMS = 128
HALF = 64
EDGE = 64
CHUNK = 128
GROUP = 8
PACKED = CHUNK + GROUP
LAG = (1, 3, 5, 8)
MESH = pl.DeviceIdType.MESH
F32, BF16 = jnp.float32, jnp.bfloat16


def keys_kernel(distance):
    m = jnp.abs(distance)
    inner = (1.5 * m - 2.5) * m * m + 1.0
    outer = ((-0.5 * m + 2.5) * m - 4.0) * m + 2.0
    return jnp.where(m < 1.0, inner, jnp.where(m < 2.0, outer, 0.0))


def split(x):
    high = x.astype(BF16)
    return high, (x - high.astype(F32)).astype(BF16)


def kernel(samples, angle_ref, shift_ref, image_ref, fraction_ref, share_ref, out_ref, cur, sent, got, own_halo,
           partner_halo, steered, w_high, w_low, rows8, taps, send_sem, recv_sem, halo_send, halo_recv):
    chunks = samples // CHUNK
    sub, rng = lax.axis_index("sub"), lax.axis_index("rng")
    ups = [lax.rem(sub // (1 << level), 2) for level in range(LEVELS)]
    partners = [sub + (1 - 2 * up) * (1 << level) for level, up in enumerate(ups)]
    other = 1 - rng

    barrier = pltpu.get_barrier_semaphore()
    neighbours = [(sub, other)] + [(p, r) for p in partners for r in (rng, other)]
    for device in neighbours:
        pl.semaphore_signal(barrier, inc=1, device_id=device, device_id_type=MESH)

    def start_row(c):
        return pl.multiple_of(jnp.where(rng == 1, c * CHUNK, samples - (c + 1) * CHUNK), CHUNK)

    for level in range(LEVELS):
        for role in range(2):
            child = ups[level] if role == 0 else 1 - ups[level]
            row = 2 * level + role
            share = share_ref[level, pl.ds(child, 1), :]
            whole = lax.rem(37 * (shift_ref[level, child, 0] + 60), 20)
            rows8[0, row : row + 1, :] = share
            rows8[1, row : row + 1, :] = whole.astype(F32) * 0.05 + 1.85 * share
    share = rows8[0]
    turns = rows8[1]
    angle = (2.0 * math.pi) * (turns - jnp.round(turns))
    rows8[2] = jnp.cos(angle) * 0.70710678
    rows8[3] = jnp.sin(angle) * 0.70710678
    sine = jnp.sin(math.pi * share)
    cosine4 = jnp.cos((math.pi / 4) * share)
    sine4 = jnp.sin((math.pi / 4) * share)
    for k in range(-4, 5):
        x = k - share
        window = 0.54 + 0.46 * (math.cos(math.pi * k / 4) * cosine4 + math.sin(math.pi * k / 4) * sine4)
        signed = sine if k % 2 else -sine
        near = x == 0.0
        sinc = jnp.where(near, 1.0, signed / (math.pi * jnp.where(near, 1.0, x)))
        taps[k + 4] = jnp.where(jnp.abs(x) < 4.0, sinc * window, 0.0)

    lane = lax.broadcasted_iota(jnp.int32, (1, BEAMS), 1)
    row128 = lax.broadcasted_iota(jnp.int32, (BEAMS, BEAMS), 0)
    row8 = lax.broadcasted_iota(jnp.int32, (GROUP, BEAMS), 0)

    def weights(level):
        up = ups[level]
        for role in range(2):
            child = up if role == 0 else 1 - up
            row = 2 * level + role
            position = 0.5 * (up * BEAMS + lane).astype(F32)
            position = position + angle_ref[level, child, 0].astype(F32) + fraction_ref[level, pl.ds(child, 1), :]
            cos, sin = rows8[2, row : row + 1, :], rows8[3, row : row + 1, :]
            if role == 0:
                keys = keys_kernel(row128.astype(F32) - position)
                top = jnp.concatenate([keys * cos, keys * sin], axis=1)
                bottom = jnp.concatenate([keys * -sin, keys * cos], axis=1)
            else:
                keys = keys_kernel((row128[:HALF] + HALF * up).astype(F32) - position)
                top = jnp.concatenate(
                    [jnp.concatenate([keys * cos, keys * sin], axis=1),
                     jnp.concatenate([keys * -sin, keys * cos], axis=1)], axis=0)
                beam = HALF - 4 * up + lax.rem(row8, 4)
                keys = keys_kernel(beam.astype(F32) - position)
                real = row8 < 4
                eight = jnp.concatenate(
                    [keys * jnp.where(real, cos, -sin), keys * jnp.where(real, sin, cos)], axis=1)
                bottom = jnp.concatenate([eight] * (BEAMS // GROUP), axis=0)
            for part, block in enumerate((top, bottom)):
                high, low = split(block)
                w_high[level, role, part * BEAMS : (part + 1) * BEAMS, :] = high
                w_low[level, role, part * BEAMS : (part + 1) * BEAMS, :] = low

    for level in range(LEVELS):
        weights(level)

    outside = pl.multiple_of(jnp.where(rng == 1, samples + EDGE, 0), EDGE)
    for level in range(LEVELS):
        for role in range(2):
            for plane in range(2):
                steered[level, role, plane, pl.ds(outside, EDGE), :] = jnp.zeros((EDGE, BEAMS), F32)

    pl.semaphore_wait(barrier, len(neighbours))

    def partner_copy(level, c):
        return pltpu.make_async_remote_copy(
            src_ref=sent.at[level, c], dst_ref=got.at[level, c], send_sem=send_sem.at[level, c],
            recv_sem=recv_sem.at[level, c], device_id=(partners[level], rng), device_id_type=MESH)

    def halo_copies(level):
        first = pl.multiple_of(jnp.where(rng == 1, 0, samples - EDGE), EDGE)
        piece = pl.multiple_of(jnp.where(rng == 1, 0, HALF), GROUP)
        return (
            pltpu.make_async_remote_copy(
                src_ref=cur.at[level, :, pl.ds(first, EDGE), :], dst_ref=own_halo.at[level],
                send_sem=halo_send.at[level, 0], recv_sem=halo_recv.at[level, 0],
                device_id=(sub, other), device_id_type=MESH),
            pltpu.make_async_remote_copy(
                src_ref=sent.at[level, 0, pl.ds(piece, EDGE + GROUP), :], dst_ref=partner_halo.at[level],
                send_sem=halo_send.at[level, 1], recv_sem=halo_recv.at[level, 1],
                device_id=(partners[level], other), device_id_type=MESH))

    def steer(level, role, x, row):
        high, low = split(x)
        wh, wl = w_high[level, role], w_low[level, role]
        s = jnp.dot(high, wh, preferred_element_type=F32)
        s = s + jnp.dot(low, wh, preferred_element_type=F32)
        s = s + jnp.dot(high, wl, preferred_element_type=F32)
        for plane in range(2):
            steered[level, role, plane, pl.ds(row, x.shape[0]), :] = s[:, plane * BEAMS : (plane + 1) * BEAMS]

    def unpack(main, margins, first_group):
        blocks = []
        for g in range(main.shape[0] // GROUP):
            blocks.append(jnp.where(lane // GROUP == first_group + g, margins, 0.0))
        return jnp.concatenate([main, jnp.concatenate(blocks, axis=0)], axis=1)

    def produce(level, c):
        row = start_row(c)
        up = ups[level]
        theirs = 1 - up
        near = cur[level, theirs, pl.ds(row, CHUNK), :]
        far = pltpu.roll(cur[level, up, pl.ds(row, CHUNK), :], HALF, 1)
        main = jnp.where((lane < HALF) == (theirs == 0), near, far)
        first = HALF - 4 * theirs
        real = cur[level, 0, pl.ds(row, CHUNK), :]
        imag = cur[level, 1, pl.ds(row, CHUNK), :]
        both = jnp.where((lane >= first) & (lane < first + 4), real, pltpu.roll(imag, 4, 1))
        margins = jnp.zeros((GROUP, BEAMS), F32)
        for g in range(CHUNK // GROUP):
            turned = pltpu.roll(both[g * GROUP : (g + 1) * GROUP], lax.rem(g * GROUP - first + BEAMS, BEAMS), 1)
            margins = jnp.where(lane // GROUP == g, turned, margins)
        sent[level, c, 0:HALF, :] = main[:HALF]
        sent[level, c, HALF : HALF + GROUP, :] = margins
        sent[level, c, HALF + GROUP : PACKED, :] = main[HALF:]
        partner_copy(level, c).start()

        @pl.when(c == 0)
        def _():
            for copy in halo_copies(level):
                copy.start()

        steer(level, 0, jnp.concatenate([real, imag], axis=1), row + EDGE)

    def steer_halo(level):
        for copy in halo_copies(level):
            copy.wait_recv()
        row = pl.multiple_of(jnp.where(rng == 1, 0, samples + EDGE), EDGE)
        steer(level, 0, jnp.concatenate([own_halo[level, 0], own_halo[level, 1]], axis=1), row)
        main = partner_halo[level, pl.ds(pl.multiple_of(rng * GROUP, GROUP), EDGE), :]
        margins = partner_halo[level, pl.ds(pl.multiple_of((1 - rng) * EDGE, GROUP), GROUP), :]
        steer(level, 1, unpack(main, margins, rng * GROUP), row)

    def merge(level, c):
        row = start_row(c)
        shifts = [shift_ref[level, ups[level] if role == 0 else 1 - ups[level], 0] for role in range(2)]
        for plane in range(2):
            total = None
            for role in range(2):
                for k in range(9):
                    weight = taps[k, 2 * level + role : 2 * level + role + 1, :]
                    term = weight * steered[level, role, plane, pl.ds(row + (EDGE - 4 + k) + shifts[role], CHUNK), :]
                    total = term if total is None else total + term
            if level + 1 < LEVELS:
                cur[level + 1, plane, pl.ds(row, CHUNK), :] = total
            else:
                out_ref[plane, :, pl.ds(row, CHUNK)] = total.T
        if level + 1 < LEVELS:
            produce(level + 1, c)

    def consume(level, c):
        @pl.when(c < chunks)
        def _():
            partner_copy(level, c).wait_recv()
            block = got[level, c]
            main = jnp.concatenate([block[:HALF], block[HALF + GROUP :]], axis=0)
            steer(level, 1, unpack(main, block[HALF : HALF + GROUP], 0), start_row(c) + EDGE)

        @pl.when(c == 0)
        def _():
            steer_halo(level)

        @pl.when(c > 0)
        def _():
            merge(level, c - 1)

    def step(k, carry):
        @pl.when(k < chunks)
        def _():
            row = start_row(k)
            for plane in range(2):
                cur[0, plane, pl.ds(row, CHUNK), :] = image_ref[plane, :, pl.ds(row, CHUNK)].T
            produce(0, k)

        for level in range(LEVELS):
            c = k - LAG[level]

            @pl.when((c >= 0) & (c <= chunks))
            def _():
                consume(level, c)

        return carry

    lax.fori_loop(0, chunks + LAG[-1] + 1, step, 0)

    def finish(c, carry):
        for level in range(LEVELS):
            partner_copy(level, c).wait_send()
        return carry

    lax.fori_loop(0, chunks, finish, 0)
    for level in range(LEVELS):
        for copy in halo_copies(level):
            copy.wait_send()


def per_device(image, angle_offset, angle_fraction, integer_distance_shifts, subcell_distance_shares):
    samples = image.shape[2]
    chunks = samples // CHUNK
    vmem, smem = pl.BlockSpec(memory_space=pltpu.VMEM), pl.BlockSpec(memory_space=pltpu.SMEM)
    return pl.pallas_call(
        lambda *refs: kernel(samples, *refs),
        out_shape=jax.ShapeDtypeStruct(image.shape, F32),
        in_specs=[smem, smem, vmem, vmem, vmem],
        out_specs=vmem,
        scratch_shapes=[
            pltpu.VMEM((LEVELS, 2, samples, BEAMS), F32),
            pltpu.VMEM((LEVELS, chunks, PACKED, BEAMS), F32),
            pltpu.VMEM((LEVELS, chunks, PACKED, BEAMS), F32),
            pltpu.VMEM((LEVELS, 2, EDGE, BEAMS), F32),
            pltpu.VMEM((LEVELS, EDGE + GROUP, BEAMS), F32),
            pltpu.VMEM((LEVELS, 2, 2, samples + 2 * EDGE, BEAMS), F32),
            pltpu.VMEM((LEVELS, 2, 2 * BEAMS, 2 * BEAMS), BF16),
            pltpu.VMEM((LEVELS, 2, 2 * BEAMS, 2 * BEAMS), BF16),
            pltpu.VMEM((4, 2 * LEVELS, BEAMS), F32),
            pltpu.VMEM((9, 2 * LEVELS, BEAMS), F32),
            pltpu.SemaphoreType.DMA((LEVELS, chunks)),
            pltpu.SemaphoreType.DMA((LEVELS, chunks)),
            pltpu.SemaphoreType.DMA((LEVELS, 2)),
            pltpu.SemaphoreType.DMA((LEVELS, 2)),
        ],
        compiler_params=pltpu.CompilerParams(
            collective_id=0, has_side_effects=True, vmem_limit_bytes=48 * 1024 * 1024),
    )(angle_offset, integer_distance_shifts, image, angle_fraction, subcell_distance_shares)


def solution(mesh):
    placed = (P(None, "sub", "rng"),) + (P(None, None, "sub"),) * 4
    return jax.shard_map(
        per_device, mesh=mesh, in_specs=placed, out_specs=P(None, "sub", "rng"), check_vma=False)
```

time: 187 us -> 61.1 us (0.33)
  waiting for transfers between devices: 103 us -> 0 us
  Pallas kernels: 0 us -> 57.9 us
  starting transfers between devices: 25.4 us -> 0 us
  between operations: 21.1 us -> 0.02 us
  other arithmetic: 15.8 us -> 0 us
  matrix products: 12.5 us -> 0 us
  local copies, waits for them, and re-layouts: 9.06 us -> 3.11 us
    ppermute x12 -> x0, waiting for transfers between devices: 103 us -> none  [the longest x4 84.9 us: from_partner(): lax.ppermute(x, axis, [(i, i ^ 1 << distance) for i in range(lax.axis_siz...]
    pallas_call x0 -> x1, Pallas kernels: none -> 57.9 us  [per_device(): pl.pallas_call(lambda *refs: kernel(samples, *refs), out_shape=jax.ShapeD...]
    ppermute x12 -> x0, starting transfers between devices: 25.4 us -> none  [the longest x4 11.4 us: extended(): lax.ppermute(tail, axis, [(i, (i + 1) % count) for i in range(ends)])]
    dot_general x8 -> x0, matrix products: 12.5 us -> none  [child_term(): jnp.einsum('ij,pjr->pir', weights, child, precision=lax.Precision.HIGHEST)]
    add x10 -> x0, other arithmetic: 9.07 us -> none  [the longest x8 8.44 us: range_shift(): summed + weight[None, :, None] * window[:, :, shift_tap:shift_tap + outpu...]
    mul x8 -> x0, other arithmetic: 4.23 us -> none  [the longest x4 3.51 us: range_shift(): weight[None, :, None] * window[:, :, shift_tap:shift_tap + output_breadth]]
    slice x6 -> x0, local copies, waits for them, and re-layouts: 2.43 us -> none  [the longest x1 1.06 us: extended(): head = lax.slice_in_dim(cells, 0, width, axis=dim)]
  transfers between devices with their start and end apart: 12 -> 0, of which waited for: 11 -> 0; matrix products, arithmetic and copies ran while one was open for 4% -> 0% of each run, Pallas kernels for 0% -> 0%
where the time goes in v1:
time: 61.1 us; the launch traced here: 61 us
  Pallas kernels  57.9 us (95%)
  local copies, waits for them, and re-layouts  3.11 us (5%)
    pallas_call x1, Pallas kernels, per_device(): pl.pallas_call(lambda *refs: kernel(samples, *refs), out_shape=jax.ShapeD...  57.9 us
    unnamed x11, local copies, waits for them, and re-layouts  3.11 us

profile of v1, /device:TPU:6, one launch (start us, length us, event | category | flops | bytes accessed | tf_op | source)
XLA Modules:
  0.0 61.0 jit_solution(5369241030566573330)
XLA Ops:
  0.0 0.0 copy-start.2
  0.0 0.0 copy-start.3
  0.0 0.0 copy-start.1
  0.0 0.8 %copy.6.refs_0_ = s32[4,2,1]{2,1,0:T(2,128)S(1)} copy(s32[4,2,1]{0,2,1:T(1,128)} %param.6) | data formatting | bytes 64 | tf_op args[1]
  0.8 0.0 copy-done.3
  0.8 0.1 copy.7.refs_1_
  0.9 0.0 copy-done.2
  0.9 0.0 copy-done.1
  0.9 0.0 copy-start
  0.9 1.2 %copy-done = f32[2,128,1024]{2,1,0:T(8,128)S(1)} copy-done((f32[2,128,1024]{2,1,0:T(8,128)S(1)}, f32[2,128,1024]{2,1,0:T(8,128)}, u32[]{:S(2)}) %copy-start) | copy-done | bytes 1048600
  2.1 57.9 %shard_map.55 = f32[2,128,1024]{2,1,0:T(8,128)S(1)} custom-call(s32[4,2,1]{2,1,0:T(2,128)S(1)} %copy.6.refs_0_, s32[4,2,1]{2,1,0:T(2,128)S(1)} %copy.7.refs_1_, f32[2,128,1024]{2,1,0:T(8,128)S(1)} %copy-done, f32[4,2,128]{2,1,0:T(2,128)S(1)} %copy-done.1, f32[4,2,128]{2,1,0:T(2,128)S(1)} %copy-done.2), custom_call_target="tpu_custom_call" | custom-call | tf_op jit(solution)/shard_map/pallas_call | solution.py:253
  60.0 1.0 %copy.9 = f32[2,128,1024]{2,1,0:T(8,128)} copy(f32[2,128,1024]{2,1,0:T(8,128)S(1)} %shard_map.55) | data formatting | bytes 2097152
Async XLA Ops:
  0.0 0.9 %copy-start.2 = (f32[4,2,128]{2,1,0:T(2,128)S(1)}, f32[4,2,128]{2,1,0:T(2,128)}, u32[]{:S(2)}) copy-start(f32[4,2,128]{2,1,0:T(2,128)} %refs_4_.1) | copy-start | bytes 12292
  0.0 0.8 %copy-start.3 = (s32[4,2,1]{0,2,1:T(1,128)S(1)}, s32[4,2,1]{0,2,1:T(1,128)}, u32[]{:S(2)}) copy-start(s32[4,2,1]{0,2,1:T(1,128)} %param.8) | copy-start | bytes 100
  0.0 0.9 %copy-start.1 = (f32[4,2,128]{2,1,0:T(2,128)S(1)}, f32[4,2,128]{2,1,0:T(2,128)}, u32[]{:S(2)}) copy-start(f32[4,2,128]{2,1,0:T(2,128)} %refs_3_.1) | copy-start | bytes 12292
  0.9 1.2 %copy-start = (f32[2,128,1024]{2,1,0:T(8,128)S(1)}, f32[2,128,1024]{2,1,0:T(8,128)}, u32[]{:S(2)}) copy-start(f32[2,128,1024]{2,1,0:T(8,128)} %refs_2_.1) | copy-start | bytes 3145732

commit v2 on v1

v2 whole, which is shorter than its diff:
```python
import math

import jax
import jax.numpy as jnp
from jax import lax
from jax.experimental import pallas as pl
from jax.experimental.pallas import tpu as pltpu
from jax.sharding import PartitionSpec as P

LEVELS = 4
BEAMS = 128
HALF = 64
EDGE = 64
CHUNK = 128
GROUP = 8
PACKED = CHUNK + GROUP
AHEAD = 2
LAG = (2, 4, 7, 10)
ORDER = (-1, 0, 1, 2, 3)
MESH = pl.DeviceIdType.MESH
F32, BF16 = jnp.float32, jnp.bfloat16


def keys_kernel(distance):
    m = jnp.abs(distance)
    inner = (1.5 * m - 2.5) * m * m + 1.0
    outer = ((-0.5 * m + 2.5) * m - 4.0) * m + 2.0
    return jnp.where(m < 1.0, inner, jnp.where(m < 2.0, outer, 0.0))


def split(x):
    high = x.astype(BF16)
    return high, (x - high.astype(F32)).astype(BF16)


def kernel(samples, angle_ref, shift_ref, image_ref, fraction_ref, share_ref, out_ref, image, cur, sent, got, own_halo,
           partner_halo, steered, weight, rows8, taps, image_sem, send_sem, recv_sem, halo_send, halo_recv):
    chunks = samples // CHUNK
    sub, rng = lax.axis_index("sub"), lax.axis_index("rng")
    ups = [lax.rem(sub // (1 << level), 2) for level in range(LEVELS)]
    partners = [sub + (1 - 2 * up) * (1 << level) for level, up in enumerate(ups)]
    other = 1 - rng

    def start_row(u, n):
        return pl.multiple_of(jnp.where(rng == 0, u, samples - u - n), HALF)

    def image_copy(c):
        return pltpu.make_async_copy(
            image_ref.at[:, :, pl.ds(pl.multiple_of(start_row(c * CHUNK, CHUNK), CHUNK), CHUNK)],
            image.at[c], image_sem.at[c])

    def out_copy(c):
        return pltpu.make_async_copy(
            image.at[c], out_ref.at[:, :, pl.ds(pl.multiple_of(start_row(c * CHUNK, CHUNK), CHUNK), CHUNK)],
            image_sem.at[c])

    for c in range(chunks):
        image_copy(c).start()

    barrier = pltpu.get_barrier_semaphore()
    neighbours = [(sub, other)] + [(p, rng) for p in partners]
    for device in neighbours:
        pl.semaphore_signal(barrier, inc=1, device_id=device, device_id_type=MESH)

    for level in range(LEVELS):
        for role in range(2):
            child = ups[level] if role == 0 else 1 - ups[level]
            row = 2 * level + role
            share = share_ref[level, pl.ds(child, 1), :]
            whole = lax.rem(37 * (shift_ref[child, 0, level] + 60), 20)
            rows8[0, row : row + 1, :] = share
            rows8[1, row : row + 1, :] = whole.astype(F32) * 0.05 + 1.85 * share
    share = rows8[0]
    turns = rows8[1]
    angle = (2.0 * math.pi) * (turns - jnp.round(turns))
    rows8[2] = jnp.cos(angle) * 0.70710678
    rows8[3] = jnp.sin(angle) * 0.70710678
    sine = jnp.sin(math.pi * share)
    cosine4 = jnp.cos((math.pi / 4) * share)
    sine4 = jnp.sin((math.pi / 4) * share)
    for k in range(-4, 5):
        x = k - share
        window = 0.54 + 0.46 * (math.cos(math.pi * k / 4) * cosine4 + math.sin(math.pi * k / 4) * sine4)
        signed = sine if k % 2 else -sine
        near = x == 0.0
        sinc = jnp.where(near, 1.0, signed / (math.pi * jnp.where(near, 1.0, x)))
        taps[k + 4] = jnp.where(jnp.abs(x) < 4.0, sinc * window, 0.0)

    lane = lax.broadcasted_iota(jnp.int32, (1, BEAMS), 1)
    row128 = lax.broadcasted_iota(jnp.int32, (BEAMS, BEAMS), 0)
    row8 = lax.broadcasted_iota(jnp.int32, (GROUP, BEAMS), 0)

    def weights(level):
        up = ups[level]
        for role in range(2):
            child = up if role == 0 else 1 - up
            row = 2 * level + role
            position = 0.5 * (up * BEAMS + lane).astype(F32)
            position = position + angle_ref[child, 0, level].astype(F32) + fraction_ref[level, pl.ds(child, 1), :]
            cos, sin = rows8[2, row : row + 1, :], rows8[3, row : row + 1, :]
            if role == 0:
                keys = keys_kernel(row128.astype(F32) - position)
                top = jnp.concatenate([keys * cos, keys * sin], axis=1)
                bottom = jnp.concatenate([keys * -sin, keys * cos], axis=1)
            else:
                keys = keys_kernel((row128[:HALF] + HALF * up).astype(F32) - position)
                top = jnp.concatenate(
                    [jnp.concatenate([keys * cos, keys * sin], axis=1),
                     jnp.concatenate([keys * -sin, keys * cos], axis=1)], axis=0)
                beam = HALF - 4 * up + lax.rem(row8, 4)
                keys = keys_kernel(beam.astype(F32) - position)
                real = row8 < 4
                eight = jnp.concatenate(
                    [keys * jnp.where(real, cos, -sin), keys * jnp.where(real, sin, cos)], axis=1)
                bottom = jnp.concatenate([eight] * (BEAMS // GROUP), axis=0)
            for part, block in enumerate((top, bottom)):
                high, low = split(block)
                for place, values in enumerate((high, high, low)):
                    first = 2 * place * BEAMS + part * BEAMS
                    weight[level, role, first : first + BEAMS, :] = values

    outside = start_row(-EDGE, EDGE) + EDGE
    for level in range(LEVELS):
        for role in range(2):
            for plane in range(2):
                steered[level, role, plane, pl.ds(outside, EDGE), :] = jnp.zeros((EDGE, BEAMS), F32)

    def partner_copy(level, c, n):
        rows = PACKED if n == CHUNK else HALF + GROUP
        return pltpu.make_async_remote_copy(
            src_ref=sent.at[level, c, 0:rows, :], dst_ref=got.at[level, c, 0:rows, :], send_sem=send_sem.at[level, c],
            recv_sem=recv_sem.at[level, c], device_id=(partners[level], rng), device_id_type=MESH)

    def halo_copies(level):
        first = start_row(samples - EDGE, EDGE)
        piece = pl.multiple_of(jnp.where(rng == 1, 0, HALF), GROUP) if level % 2 == 0 else 0
        return (
            pltpu.make_async_remote_copy(
                src_ref=cur.at[level, :, pl.ds(first, EDGE), :], dst_ref=own_halo.at[level],
                send_sem=halo_send.at[level, 0], recv_sem=halo_recv.at[level, 0],
                device_id=(sub, other), device_id_type=MESH),
            pltpu.make_async_remote_copy(
                src_ref=sent.at[level, chunks - 1 + level % 2, pl.ds(piece, EDGE + GROUP), :], dst_ref=partner_halo.at[level],
                send_sem=halo_send.at[level, 1], recv_sem=halo_recv.at[level, 1],
                device_id=(partners[level], other), device_id_type=MESH))

    def steer(level, role, x, row):
        high, low = split(x)
        s = jnp.dot(jnp.concatenate([high, low, high], axis=1), weight[level, role], preferred_element_type=F32)
        for plane in range(2):
            steered[level, role, plane, pl.ds(row, x.shape[0]), :] = s[:, plane * BEAMS : (plane + 1) * BEAMS]

    def unpack(main, margins, first_group):
        blocks = []
        for g in range(main.shape[0] // GROUP):
            blocks.append(jnp.where(lane // GROUP == first_group + g, margins, 0.0))
        return jnp.concatenate([main, jnp.concatenate(blocks, axis=0)], axis=1)

    def produce(level, c, u, n, send=True):
        row = start_row(u, n)
        up = ups[level]
        theirs = 1 - up
        near = cur[level, theirs, pl.ds(row, n), :]
        far = pltpu.roll(cur[level, up, pl.ds(row, n), :], HALF, 1)
        main = jnp.where((lane < HALF) == (theirs == 0), near, far)
        first = HALF - 4 * theirs
        real = cur[level, 0, pl.ds(row, n), :]
        imag = cur[level, 1, pl.ds(row, n), :]
        both = jnp.where((lane >= first) & (lane < first + 4), real, pltpu.roll(imag, 4, 1))
        margins = jnp.zeros((GROUP, BEAMS), F32)
        for g in range(n // GROUP):
            turned = pltpu.roll(both[g * GROUP : (g + 1) * GROUP], lax.rem(g * GROUP - first + BEAMS, BEAMS), 1)
            margins = jnp.where(lane // GROUP == g, turned, margins)
        sent[level, c, 0:HALF, :] = main[:HALF]
        sent[level, c, HALF : HALF + GROUP, :] = margins
        if n == CHUNK:
            sent[level, c, HALF + GROUP : PACKED, :] = main[HALF:]
        if send:
            send_out(level, c, n)

    def send_out(level, c, n):
        partner_copy(level, c, n).start()

        def halos():
            for copy in halo_copies(level):
                copy.start()

        if level % 2 == 0:
            if not isinstance(c, int):
                pl.when(c == chunks - 1)(halos)
        elif isinstance(c, int) and c == chunks:
            halos()

    def steer_halo(level):
        for copy in halo_copies(level):
            copy.wait_recv()
        row = start_row(samples, EDGE) + EDGE
        steer(level, 0, jnp.concatenate([own_halo[level, 0], own_halo[level, 1]], axis=1), row)
        if level % 2 == 0:
            main = partner_halo[level, pl.ds(pl.multiple_of(rng * GROUP, GROUP), EDGE), :]
            margins = partner_halo[level, pl.ds(pl.multiple_of((1 - rng) * EDGE, GROUP), GROUP), :]
            steer(level, 1, unpack(main, margins, rng * GROUP), row)
        else:
            steer(level, 1, unpack(partner_halo[level, 0:EDGE, :], partner_halo[level, EDGE:, :], 0), row)

    def shifted(level, role, plane, row, n):
        start = row + (EDGE - 4) + shift_ref[ups[level] if role == 0 else 1 - ups[level], 0, level]
        total = None
        for k in range(9):
            tap = taps[k, 2 * level + role : 2 * level + role + 1, :]
            term = tap * steered[level, role, plane, pl.ds(start + k, n), :]
            total = term if total is None else total + term
        return total

    def merge_own(level, u, n):
        row = start_row(u, n)
        for plane in range(2):
            cur[level + 1, plane, pl.ds(row, n), :] = shifted(level, 0, plane, row, n)

    def merge(level, c, u, n):
        row = start_row(u, n)
        for plane in range(2):
            total = cur[level + 1, plane, pl.ds(row, n), :] + shifted(level, 1, plane, row, n)
            if level + 1 < LEVELS:
                cur[level + 1, plane, pl.ds(row, n), :] = total
            else:
                image[c, plane] = total.T
        if level + 1 < LEVELS:
            produce(level + 1, c, u, n)
        else:
            out_copy(c).start()

    def steer_own(level, u, n):
        row = start_row(u, n)
        own = [cur[level, plane, pl.ds(row, n), :] for plane in range(2)]
        steer(level, 0, jnp.concatenate(own, axis=1), row + EDGE)

    def receive(level, c, u, n):
        partner_copy(level, c, n).wait_recv()
        margins = got[level, c, HALF : HALF + GROUP, :]
        main = got[level, c, 0:HALF, :]
        if n == CHUNK:
            main = jnp.concatenate([main, got[level, c, HALF + GROUP : PACKED, :]], axis=0)
        steer(level, 1, unpack(main, margins, 0), start_row(u, n) + EDGE)

    def consume(level, c):
        if level % 2 == 0:
            steer_own(level, c * CHUNK, CHUNK)

            @pl.when(c == 0)
            def _():
                merge_own(level, 0, HALF)
                receive(level, 0, 0, CHUNK)
                merge(level, 0, 0, HALF)

            @pl.when(c > 0)
            def _():
                merge_own(level, c * CHUNK - HALF, CHUNK)
                receive(level, c, c * CHUNK, CHUNK)
                merge(level, c, c * CHUNK - HALF, CHUNK)

            @pl.when(c == chunks - 1)
            def _():
                steer_halo(level)
                merge_own(level, samples - HALF, HALF)
                merge(level, chunks, samples - HALF, HALF)
        else:
            @pl.when(c == 0)
            def _():
                steer_own(level, 0, HALF)
                receive(level, 0, 0, HALF)

            @pl.when((c > 0) & (c < chunks))
            def _():
                steer_own(level, c * CHUNK - HALF, CHUNK)
                merge_own(level, (c - 1) * CHUNK, CHUNK)
                receive(level, c, c * CHUNK - HALF, CHUNK)

            @pl.when(c == chunks)
            def _():
                steer_own(level, samples - HALF, HALF)
                steer_halo(level)
                merge_own(level, samples - CHUNK, CHUNK)
                receive(level, chunks, samples - HALF, HALF)

            @pl.when(c > 0)
            def _():
                merge(level, c - 1, (c - 1) * CHUNK, CHUNK)

    def take(c, send=True):
        image_copy(c).wait()
        row = start_row(c * CHUNK, CHUNK)
        for plane in range(2):
            cur[0, plane, pl.ds(row, CHUNK), :] = image[c, plane].T
        produce(0, c, c * CHUNK, CHUNK, send)

    for c in range(AHEAD):
        take(c, False)
    weights(0)
    pl.semaphore_wait(barrier, len(neighbours))
    for c in range(AHEAD):
        send_out(0, c, CHUNK)
    for level in range(1, LEVELS):
        weights(level)

    def step(k, carry):
        for level in ORDER:
            if level < 0:
                pl.when(k < chunks)(lambda: take(k))
            else:
                c = k - LAG[level]
                pl.when((c >= 0) & (c < chunks + level % 2))(lambda level=level, c=c: consume(level, c))
        return carry

    lax.fori_loop(AHEAD, chunks + LAG[-1] + 1, step, 0)

    for level in range(LEVELS):
        first = level % 2

        def finish(c, carry):
            partner_copy(level, c, CHUNK).wait_send()
            return carry

        lax.fori_loop(first, chunks, finish, 0)
        if first:
            partner_copy(level, 0, HALF).wait_send()
            partner_copy(level, chunks, HALF).wait_send()
        for copy in halo_copies(level):
            copy.wait_send()
    for c in range(chunks):
        out_copy(c).wait()


def per_device(image, angle_offset, angle_fraction, integer_distance_shifts, subcell_distance_shares):
    samples = image.shape[2]
    chunks = samples // CHUNK
    vmem, smem = pl.BlockSpec(memory_space=pltpu.VMEM), pl.BlockSpec(memory_space=pltpu.SMEM)
    return pl.pallas_call(
        lambda *refs: kernel(samples, *refs),
        out_shape=jax.ShapeDtypeStruct(image.shape, F32),
        in_specs=[smem, smem, pl.BlockSpec(memory_space=pltpu.HBM), vmem, vmem],
        out_specs=pl.BlockSpec(memory_space=pltpu.HBM),
        scratch_shapes=[
            pltpu.VMEM((chunks, 2, BEAMS, CHUNK), F32),
            pltpu.VMEM((LEVELS + 1, 2, samples, BEAMS), F32),
            pltpu.VMEM((LEVELS, chunks + 1, PACKED, BEAMS), F32),
            pltpu.VMEM((LEVELS, chunks + 1, PACKED, BEAMS), F32),
            pltpu.VMEM((LEVELS, 2, EDGE, BEAMS), F32),
            pltpu.VMEM((LEVELS, EDGE + GROUP, BEAMS), F32),
            pltpu.VMEM((LEVELS, 2, 2, samples + 2 * EDGE, BEAMS), F32),
            pltpu.VMEM((LEVELS, 2, 6 * BEAMS, 2 * BEAMS), BF16),
            pltpu.VMEM((4, 2 * LEVELS, BEAMS), F32),
            pltpu.VMEM((9, 2 * LEVELS, BEAMS), F32),
            pltpu.SemaphoreType.DMA((chunks,)),
            pltpu.SemaphoreType.DMA((LEVELS, chunks + 1)),
            pltpu.SemaphoreType.DMA((LEVELS, chunks + 1)),
            pltpu.SemaphoreType.DMA((LEVELS, 2)),
            pltpu.SemaphoreType.DMA((LEVELS, 2)),
        ],
        compiler_params=pltpu.CompilerParams(
            collective_id=0, has_side_effects=True, vmem_limit_bytes=56 * 1024 * 1024),
    )(jnp.transpose(angle_offset, (1, 2, 0)), jnp.transpose(integer_distance_shifts, (1, 2, 0)), image, angle_fraction, subcell_distance_shares)


def solution(mesh):
    placed = (P(None, "sub", "rng"),) + (P(None, None, "sub"),) * 4
    return jax.shard_map(
        per_device, mesh=mesh, in_specs=placed, out_specs=P(None, "sub", "rng"), check_vma=False)
```

time: 61.1 us -> 53.3 us (0.87)
  Pallas kernels: 57.9 us -> 50.8 us
  local copies, waits for them, and re-layouts: 3.11 us -> 2.31 us
    pallas_call x1, Pallas kernels: 57.9 us -> 50.8 us  [per_device(): pl.pallas_call(lambda *refs: kernel(samples, *refs), out_shape=jax.ShapeD...]
    unnamed x11 -> x1, local copies, waits for them, and re-layouts: 3.11 us -> 2.31 us
where the time goes in v2:
time: 53.3 us; the launch traced here: 53.1 us
  Pallas kernels  50.8 us (95%)
  local copies, waits for them, and re-layouts  2.31 us (4%)
    pallas_call x1, Pallas kernels, per_device(): pl.pallas_call(lambda *refs: kernel(samples, *refs), out_shape=jax.ShapeD...  50.8 us
    unnamed x1, local copies, waits for them, and re-layouts  2.31 us

profile of v2, /device:TPU:6, one launch (start us, length us, event | category | flops | bytes accessed | tf_op | source)
XLA Modules:
  0.0 53.1 jit_solution(1497533242175180932)
XLA Ops:
  0.0 50.8 %shard_map.55 = f32[2,128,1024]{2,1,0:T(8,128)} custom-call(s32[2,1,4]{2,1,0:T(1,128)} %bitcast.2, s32[2,1,4]{2,1,0:T(1,128)} %bitcast.3, f32[2,128,1024]{2,1,0:T(8,128)} %refs_2_.1, f32[4,2,128]{2,1,0:T(2,128)} %refs_3_.1, f32[4,2,128]{2,1,0:T(2,128)} %refs_4_.1), custom_call_target="tpu_custom_call" | custom-call | tf_op jit(solution)/shard_map/pallas_call | solution.py:338
  50.8 2.3 %copy.7 = f32[2,128,1024]{2,1,0:T(8,128)} copy(f32[2,128,1024]{2,1,0:T(8,128)} %shard_map.55) | data formatting | bytes 2097152

commit v3 on v2

--- a/solution.py
+++ b/solution.py
@@ -15,8 +15,9 @@
 GROUP = 8
 PACKED = CHUNK + GROUP
 AHEAD = 2
-LAG = (2, 4, 7, 10)
-ORDER = (-1, 0, 1, 2, 3)
+LAG = (2, 3, 6, 10)
+WEIGHTS = {1: (3, 2), 2: (5, 3)}
+ORDER = (0, -1, 1, 2, 3)
 MESH = pl.DeviceIdType.MESH
 F32, BF16 = jnp.float32, jnp.bfloat16
 
@@ -300,11 +301,12 @@
     pl.semaphore_wait(barrier, len(neighbours))
     for c in range(AHEAD):
         send_out(0, c, CHUNK)
-    for level in range(1, LEVELS):
-        weights(level)
+    weights(1)
 
     def step(k, carry):
         for level in ORDER:
+            if level in WEIGHTS:
+                pl.when(k == WEIGHTS[level][0])(lambda level=level: weights(WEIGHTS[level][1]))
             if level < 0:
                 pl.when(k < chunks)(lambda: take(k))
             else:

time: 53.3 us -> 53.1 us (level)
  no operation moved by 1% of the time
where the time goes in v3:
time: 53.1 us; the launch traced here: 52.7 us
  Pallas kernels  50.4 us (95%)
  local copies, waits for them, and re-layouts  2.31 us (4%)
    pallas_call x1, Pallas kernels, per_device(): pl.pallas_call(lambda *refs: kernel(samples, *refs), out_shape=jax.ShapeD...  50.4 us
    unnamed x1, local copies, waits for them, and re-layouts  2.31 us

profile of v3, /device:TPU:6, one launch (start us, length us, event | category | flops | bytes accessed | tf_op | source)
XLA Modules:
  0.0 52.7 jit_solution(3050596643713579340)
XLA Ops:
  0.0 50.4 %shard_map.55 = f32[2,128,1024]{2,1,0:T(8,128)} custom-call(s32[2,1,4]{2,1,0:T(1,128)} %bitcast.2, s32[2,1,4]{2,1,0:T(1,128)} %bitcast.3, f32[2,128,1024]{2,1,0:T(8,128)} %refs_2_.1, f32[4,2,128]{2,1,0:T(2,128)} %refs_3_.1, f32[4,2,128]{2,1,0:T(2,128)} %refs_4_.1), custom_call_target="tpu_custom_call" | custom-call | tf_op jit(solution)/shard_map/pallas_call | solution.py:340
  50.4 2.3 %copy.7 = f32[2,128,1024]{2,1,0:T(8,128)} copy(f32[2,128,1024]{2,1,0:T(8,128)} %shard_map.55) | data formatting | bytes 2097152

commit v4 on v3

--- a/solution.py
+++ b/solution.py
@@ -135,15 +135,19 @@
     def halo_copies(level):
         first = start_row(samples - EDGE, EDGE)
         piece = pl.multiple_of(jnp.where(rng == 1, 0, HALF), GROUP) if level % 2 == 0 else 0
+        if level == LEVELS - 1:
+            source, target = got.at[level, chunks, 0 : EDGE + GROUP, :], sub
+        else:
+            source, target = sent.at[level, chunks - 1 + level % 2, pl.ds(piece, EDGE + GROUP), :], partners[level]
         return (
             pltpu.make_async_remote_copy(
                 src_ref=cur.at[level, :, pl.ds(first, EDGE), :], dst_ref=own_halo.at[level],
                 send_sem=halo_send.at[level, 0], recv_sem=halo_recv.at[level, 0],
                 device_id=(sub, other), device_id_type=MESH),
             pltpu.make_async_remote_copy(
-                src_ref=sent.at[level, chunks - 1 + level % 2, pl.ds(piece, EDGE + GROUP), :], dst_ref=partner_halo.at[level],
+                src_ref=source, dst_ref=partner_halo.at[level],
                 send_sem=halo_send.at[level, 1], recv_sem=halo_recv.at[level, 1],
-                device_id=(partners[level], other), device_id_type=MESH))
+                device_id=(target, other), device_id_type=MESH))
 
     def steer(level, role, x, row):
         high, low = split(x)
@@ -183,7 +187,7 @@
         partner_copy(level, c, n).start()
 
         def halos():
-            for copy in halo_copies(level):
+            for copy in halo_copies(level)[: 1 if level == LEVELS - 1 else 2]:
                 copy.start()
 
         if level % 2 == 0:
@@ -236,14 +240,26 @@
         own = [cur[level, plane, pl.ds(row, n), :] for plane in range(2)]
         steer(level, 0, jnp.concatenate(own, axis=1), row + EDGE)
 
-    def receive(level, c, u, n):
-        partner_copy(level, c, n).wait_recv()
+    def receive(level, c, u, n, here=False):
+        if not here:
+            partner_copy(level, c, n).wait_recv()
         margins = got[level, c, HALF : HALF + GROUP, :]
         main = got[level, c, 0:HALF, :]
         if n == CHUNK:
             main = jnp.concatenate([main, got[level, c, HALF + GROUP : PACKED, :]], axis=0)
         steer(level, 1, unpack(main, margins, 0), start_row(u, n) + EDGE)
 
+    def consume_last(level, before_wait=lambda: None):
+        steer_own(level, samples - HALF, HALF)
+        steer_halo(level)
+        merge_own(level, samples - CHUNK, CHUNK)
+        before_wait()
+        receive(level, chunks, samples - HALF, HALF, here=level == LEVELS - 1)
+
+    def hand_on():
+        partner_copy(LEVELS - 1, chunks, HALF).wait_recv()
+        halo_copies(LEVELS - 1)[1].start()
+
     def consume(level, c):
         if level % 2 == 0:
             steer_own(level, c * CHUNK, CHUNK)
@@ -254,7 +270,7 @@
                 receive(level, 0, 0, CHUNK)
                 merge(level, 0, 0, HALF)
 
-            @pl.when(c > 0)
+            @pl.when((c > 0) & (c < chunks - 1))
             def _():
                 merge_own(level, c * CHUNK - HALF, CHUNK)
                 receive(level, c, c * CHUNK, CHUNK)
@@ -262,9 +278,15 @@
 
             @pl.when(c == chunks - 1)
             def _():
+                merge_own(level, c * CHUNK - HALF, CHUNK)
+                receive(level, c, c * CHUNK, CHUNK)
+                if level == 0:
+                    merge(level, c, c * CHUNK - HALF, CHUNK)
                 steer_halo(level)
                 merge_own(level, samples - HALF, HALF)
                 merge(level, chunks, samples - HALF, HALF)
+                if level != 0:
+                    merge(level, c, c * CHUNK - HALF, CHUNK)
         else:
             @pl.when(c == 0)
             def _():
@@ -275,14 +297,12 @@
             def _():
                 steer_own(level, c * CHUNK - HALF, CHUNK)
                 merge_own(level, (c - 1) * CHUNK, CHUNK)
+                if level == LEVELS - 1:
+                    pl.when(c == chunks - 1)(hand_on)
                 receive(level, c, c * CHUNK - HALF, CHUNK)
 
-            @pl.when(c == chunks)
-            def _():
-                steer_own(level, samples - HALF, HALF)
-                steer_halo(level)
-                merge_own(level, samples - CHUNK, CHUNK)
-                receive(level, chunks, samples - HALF, HALF)
+            if level < LEVELS - 1:
+                pl.when(c == chunks)(lambda: consume_last(level))
 
             @pl.when(c > 0)
             def _():
@@ -311,26 +331,36 @@
                 pl.when(k < chunks)(lambda: take(k))
             else:
                 c = k - LAG[level]
-                pl.when((c >= 0) & (c < chunks + level % 2))(lambda level=level, c=c: consume(level, c))
+                last = chunks + (level == 1)
+                pl.when((c >= 0) & (c < last))(lambda level=level, c=c: consume(level, c))
         return carry
 
-    lax.fori_loop(AHEAD, chunks + LAG[-1] + 1, step, 0)
-
-    for level in range(LEVELS):
-        first = level % 2
-
-        def finish(c, carry):
-            partner_copy(level, c, CHUNK).wait_send()
-            return carry
-
-        lax.fori_loop(first, chunks, finish, 0)
-        if first:
-            partner_copy(level, 0, HALF).wait_send()
-            partner_copy(level, chunks, HALF).wait_send()
-        for copy in halo_copies(level):
-            copy.wait_send()
-    for c in range(chunks):
-        out_copy(c).wait()
+    lax.fori_loop(AHEAD, chunks + LAG[-1], step, 0)
+
+    def sent_all(levels):
+        for level in levels:
+            first = level % 2
+
+            def finish(c, carry):
+                partner_copy(level, c, CHUNK).wait_send()
+                return carry
+
+            lax.fori_loop(first, chunks, finish, 0)
+            if first:
+                partner_copy(level, 0, HALF).wait_send()
+                partner_copy(level, chunks, HALF).wait_send()
+            for copy in halo_copies(level):
+                copy.wait_send()
+
+    def before_wait():
+        sent_all(range(LEVELS - 1))
+        for c in range(chunks - 1):
+            out_copy(c).wait()
+
+    consume_last(LEVELS - 1, before_wait)
+    merge(LEVELS - 1, chunks - 1, samples - CHUNK, CHUNK)
+    sent_all((LEVELS - 1,))
+    out_copy(chunks - 1).wait()
 
 
 def per_device(image, angle_offset, angle_fraction, integer_distance_shifts, subcell_distance_shares):

time: 53.1 us -> 53.1 us (level)
  no operation moved by 1% of the time
where the time goes in v4:
time: 53.1 us; the launch traced here: 52.4 us
  Pallas kernels  50.1 us (94%)
  local copies, waits for them, and re-layouts  2.31 us (4%)
    pallas_call x1, Pallas kernels, per_device(): pl.pallas_call(lambda *refs: kernel(samples, *refs), out_shape=jax.ShapeD...  50.1 us
    unnamed x1, local copies, waits for them, and re-layouts  2.31 us

profile of v4, /device:TPU:6, one launch (start us, length us, event | category | flops | bytes accessed | tf_op | source)
XLA Modules:
  0.0 52.4 jit_solution(17925074439656060950)
XLA Ops:
  0.0 50.1 %shard_map.55 = f32[2,128,1024]{2,1,0:T(8,128)} custom-call(s32[2,1,4]{2,1,0:T(1,128)} %bitcast.2, s32[2,1,4]{2,1,0:T(1,128)} %bitcast.3, f32[2,128,1024]{2,1,0:T(8,128)} %refs_2_.1, f32[4,2,128]{2,1,0:T(2,128)} %refs_3_.1, f32[4,2,128]{2,1,0:T(2,128)} %refs_4_.1), custom_call_target="tpu_custom_call" | custom-call | tf_op jit(solution)/shard_map/pallas_call | solution.py:370
  50.1 2.3 %copy.7 = f32[2,128,1024]{2,1,0:T(8,128)} copy(f32[2,128,1024]{2,1,0:T(8,128)} %shard_map.55) | data formatting | bytes 2097152
